TPU v7x, 256 devices: a whole 4x4x8 slice. The times are simulated.
256 devices in a mesh: particle: 8 (over x, z_hi), domain: 32 (over z_lo, y, core).
Axes of the slice: x: 4, y: 4, z: 8 (z_hi: 2, z_lo: 4; z = z_hi * 4 + z_lo), core: 2. Of those that a mesh axis runs over, the one named last changes fastest.
Arguments:
- states: float32 [32, 20, 256, 1024], P('particle', None, 'domain'), may hold values from -6 to 6
- parents: int32 [32], P('particle'), may hold values from 0 to 31
- perturbation: float32 [32, 20, 256, 1024], P('particle', None, 'domain'), may hold values from -4 to 4
- sea_mask: int32 [256, 1024], P('domain'), may hold values 0 or 1
- diffusivity: float32 [20], replicated, may hold values from 0.02 to 0.24
- coupling: float32 [20, 20], replicated, may hold values from -1.25 to 1.25
Outputs:
- forecast: float32 [32, 20, 256, 1024], P('particle', None, 'domain')
All inputs are finite; a program needn't handle non-finite values. No bound on the sum of `sea_mask` on one device may be relied on, other than what follows from the above.
Results may differ from a plain program's by a relative error of at most 0.00009.
Values sent between devices are 32-bit elements; how exact they have to be, the bound alone decides.
A program may use at most 128 MiB of HBM per device.

v0:
```python
import jax
import jax.numpy as jnp
from jax import lax
from jax.sharding import PartitionSpec as P


def with_halo(block, sides, width):
    for axis, dim in sides:
        count = lax.axis_size(axis)
        forward = [(i, i + 1) for i in range(count - 1)]
        backward = [(target, source) for source, target in forward]
        low = lax.ppermute(
            lax.slice_in_dim(block, block.shape[dim] - width, None, axis=dim), axis, forward
        )
        high = lax.ppermute(lax.slice_in_dim(block, 0, width, axis=dim), axis, backward)
        block = jnp.concatenate([low, block, high], axis=dim)
    return block


def advance(padded, mask_rows, diffusivity, coupling):
    center = padded[:, :, 1:-1]
    laplace = (
        padded[:, :, :-2]
        + padded[:, :, 2:]
        + jnp.roll(center, 1, 3)
        + jnp.roll(center, -1, 3)
        - 4.0 * center
    )
    coupled = jnp.einsum("cd,pdrl->pcrl", coupling, center, precision=lax.Precision.HIGHEST)
    return center + mask_rows[None, None] * (diffusivity[None, :, None, None] * laplace + coupled)


def on_device(states, parents, perturbation, sea_mask, diffusivity, coupling):
    shard_rows = lax.all_gather(states, "particle", axis=0, tiled=True)
    labels = jnp.arange(shard_rows.shape[0], dtype=jnp.int32)
    chosen = (parents[:, None] == labels[None, :]).astype(jnp.float32)
    resampled = jnp.einsum("ji,icrl->jcrl", chosen, shard_rows, precision=lax.Precision.HIGHEST)
    resampled = resampled + perturbation
    mask_rows = sea_mask.astype(jnp.float32)
    fields = resampled
    for sweep in range(2):
        padded = with_halo(fields, (("domain", 2),), 1)
        fields = advance(padded, mask_rows, diffusivity, coupling)
    return fields


def solution(mesh):
    in_specs = (
        P("particle", None, "domain", None),
        P("particle"),
        P("particle", None, "domain", None),
        P("domain", None),
        P(),
        P(),
    )
    out_specs = P("particle", None, "domain", None)
    return jax.shard_map(
        on_device, mesh=mesh, in_specs=in_specs, out_specs=out_specs, check_vma=False
    )
```

profile of v0, /device:TPU:25, one launch (start us, length us, event | category | flops | bytes accessed | tf_op | source)
XLA Modules:
  0.0 462.8 jit_solution(8590281608015983270)
XLA Ops:
  6.5 0.0 copy-start
  6.5 0.0 all-gather.2.cloned.1.call-start
  6.6 0.7 all-gather.2.cloned.1.call-update
  7.3 0.0 copy-done.2
  7.3 379.2 %all-gather.2.cloned.1.call-done = f32[32,20,8,1024]{3,2,1,0:T(8,128)} async-done(((f32[4,20,8,1024]{3,2,1,0:T(8,128)}), f32[32,20,8,1024]{3,2,1,0:T(8,128)}) %all-gather.2.cloned.1.call-update) | async-done | bytes 20971536 | tf_op jit(solution)/shard_map/all_gather | solution.py:34
  386.5 27.1 %copy_add_fusion = f32[4,20,8,1024]{3,0,2,1:T(4,128)S(1)} fusion(f32[4,20,8,1024]{3,2,1,0:T(8,128)S(1)} %copy-done.1, f32[32,20,8,1024]{3,2,1,0:T(8,128)} %all-gather.2.cloned.1.call-done, s32[4]{0:T(128)S(1)} %copy-done.4), kind=kOutput, calls=%fused_computation.26 | convolution fusion | flops 252313728 | bytes 26214416 | tf_op jit(solution)/shard_map/ji,icrl->jcrl/dot_general | solution.py:37
  413.6 0.2 fusion.33
  413.9 2.1 fusion.32
  416.0 1.9 collective-permute-start
  417.9 0.0 copy-start.3
  417.9 3.0 collective-permute-start.1
  421.0 5.7 %fusion.4 = f32[4,8,1024,20]{2,3,1,0:T(8,128)S(1)} fusion(f32[4,20,8,1024]{3,0,2,1:T(4,128)S(1)} %copy_add_fusion, f32[20,20]{1,0:T(8,128)S(1)} %copy-done), kind=kOutput, calls=%fused_computation.4 | convolution fusion | flops 157286400 | bytes 5244480 | tf_op jit(solution)/shard_map/cd,pdrl->pcrl/dot_general | solution.py:29
  426.7 0.0 collective-permute-done
  426.7 1.8 collective-permute-done.1
  428.4 4.4 fusion.21
  432.8 0.2 fusion.30
  433.1 2.0 fusion.29
  435.1 3.0 collective-permute-start.2
  438.1 2.1 collective-permute-start.3
  440.2 5.7 %fusion.2 = f32[4,8,1024,20]{2,3,1,0:T(8,128)S(1)} fusion(f32[4,20,8,1024]{3,0,2,1:T(4,128)S(1)} %fusion.21, f32[20,20]{1,0:T(8,128)S(1)} %copy-done), kind=kOutput, calls=%fused_computation.2 | convolution fusion | flops 157286400 | bytes 5244480 | tf_op jit(solution)/shard_map/cd,pdrl->pcrl/dot_general | solution.py:29
  445.9 0.0 collective-permute-done.2
  445.9 2.7 collective-permute-done.3
  448.6 4.4 fusion.13
  453.0 3.0 copy.20
  (10 shorter events, 0.1 us)
Async XLA Ops:
  6.5 414.4 %copy-start = (f32[20,20]{1,0:T(8,128)S(1)}, f32[20,20]{1,0:T(8,128)}, u32[]{:S(2)}) copy-start(f32[20,20]{1,0:T(8,128)} %param.11) | copy-start | bytes 4804
  6.5 0.8 copy-start.2
  6.5 380.0 %copy-start.1 = (f32[4,20,8,1024]{3,2,1,0:T(8,128)S(1)}, f32[4,20,8,1024]{3,2,1,0:T(8,128)}, u32[]{:S(2)}) copy-start(f32[4,20,8,1024]{3,2,1,0:T(8,128)} %param.8) | copy-start | bytes 7864324
  6.5 380.0 %copy-start.4 = (s32[4]{0:T(128)S(1)}, s32[4]{0:T(128)}, u32[]{:S(2)}) copy-start(s32[4]{0:T(128)} %param.7) | copy-start | bytes 52
  6.5 380.0 %all-gather.2.cloned.1.call-start = ((), (), s32[]{:S(2)}) async-start(), calls=%async_computation | async-start | bytes 23592960 | tf_op jit(solution)/shard_map/all_gather | solution.py:34
  416.0 10.7 %collective-permute-start = (f32[4,20,1,1024]{3,0,2,1:T(4,128)S(1)}, f32[4,20,1,1024]{3,0,2,1:T(4,128)S(1)}, u32[]{:S(2)}, u32[]{:S(2)}) collective-permute-start(f32[4,20,1,1024]{3,0,2,1:T(4,128)S(1)} %get-tuple-element.15), channel_id=1, source_target_pairs={{0,1},{1,2},{2,3},{3,4},{4,5},{5,6},{6,7},{7,8},{8,9},{9,10},{10,1... | collective-permute-start | bytes 983048 | tf_op jit(solution)/shard_map/ppermute | solution.py:12
  417.9 10.5 %copy-start.3 = (f32[20]{0:T(128)S(1)}, f32[20]{0:T(128)}, u32[]{:S(2)}) copy-start(f32[20]{0:T(128)} %param.10) | copy-start | bytes 244
  417.9 10.5 %collective-permute-start.1 = (f32[4,20,1,1024]{3,0,2,1:T(4,128)S(1)}, f32[4,20,1,1024]{3,0,2,1:T(4,128)S(1)}, u32[]{:S(2)}, u32[]{:S(2)}) collective-permute-start(f32[4,20,1,1024]{3,0,2,1:T(4,128)S(1)} %get-tuple-element.16), channel_id=1, source_target_pairs={{1,0},{2,1},{3,2},{4,3},{5,4},{6,5},{7,6},{8,7},{9,8},{10,9},{11,1... | collective-permute-start | bytes 983048 | tf_op jit(solution)/shard_map/ppermute | solution.py:15
  435.1 10.8 %collective-permute-start.2 = (f32[4,20,1,1024]{3,0,2,1:T(4,128)S(1)}, f32[4,20,1,1024]{3,0,2,1:T(4,128)S(1)}, u32[]{:S(2)}, u32[]{:S(2)}) collective-permute-start(f32[4,20,1,1024]{3,0,2,1:T(4,128)S(1)} %get-tuple-element.9), channel_id=1, source_target_pairs={{0,1},{1,2},{2,3},{3,4},{4,5},{5,6},{6,7},{7,8},{8,9},{9,10},{10,1... | collective-permute-start | bytes 983048 | tf_op jit(solution)/shard_map/ppermute | solution.py:12
  438.1 10.5 %collective-permute-start.3 = (f32[4,20,1,1024]{3,0,2,1:T(4,128)S(1)}, f32[4,20,1,1024]{3,0,2,1:T(4,128)S(1)}, u32[]{:S(2)}, u32[]{:S(2)}) collective-permute-start(f32[4,20,1,1024]{3,0,2,1:T(4,128)S(1)} %get-tuple-element.10), channel_id=1, source_target_pairs={{1,0},{2,1},{3,2},{4,3},{5,4},{6,5},{7,6},{8,7},{9,8},{10,9},{11,1... | collective-permute-start | bytes 983048 | tf_op jit(solution)/shard_map/ppermute | solution.py:15
Sparse Core Ops, SparseCore 0:
  10.0 376.4 all-gather.1
where the time goes:
time: 463 us
  waiting for transfers between devices  384 us (83%)
  matrix products  38.4 us (8%)
  between operations  13.5 us (3%)
  starting transfers between devices  10.1 us (2%)
  other arithmetic  8.74 us (2%)
  local copies, waits for them, and re-layouts  7.74 us (2%)
    all_gather x1, waiting for transfers between devices, on_device(): shard_rows = lax.all_gather(states, 'particle', axis=0, tiled=True)  379 us
    dot_general x1, matrix products, on_device(): jnp.einsum('ji,icrl->jcrl', chosen, shard_rows, precision=lax.Precision.H...  27.1 us
    dot_general x2, matrix products, advance(): jnp.einsum('cd,pdrl->pcrl', coupling, center, precision=lax.Precision.HIG...  11.4 us
  transfers between devices with their start and end apart: 5, of which 3 were waited for; matrix products, arithmetic and copies ran while one was open for 2% of the time, Pallas kernels for 0%

commit v1 on v0

v1 whole, which is shorter than its diff:
```python
import functools
import jax
import jax.numpy as jnp
from jax import lax
from jax.experimental import pallas as pl
from jax.experimental.pallas import tpu as pltpu
from jax.sharding import PartitionSpec as P

MESH = pl.DeviceIdType.MESH
CH, LON, ROWS = 20, 1024, 8
GROUP = 5
HALF = 16
CAP = 8
CHUNKS = 8
WIDTH = LON // CHUNKS
AHEAD = 3
WIN = 24


def route(states, pert, parents, mask, res, halo, mask_halo, flag, *scratch):
    it = iter(scratch)
    take = lambda: [next(it) for _ in range(CHUNKS)]
    mine, crossing, crossed, back, got = take(), take(), take(), take(), take()
    edge = take()
    (pert_v, strip, par_send, par_x, par_z, par_xs, par_zs, bits, table, listed) = (next(it) for _ in range(10))
    (s_x1, r_x1, l_x1, s_z, r_z, s_x2, r_x2, s_h, r_h, s_p, r_p, s_q, r_q, s_m, r_m, l_c) = (
        next(it) for _ in range(16)
    )
    p, dom = lax.axis_index("particle"), lax.axis_index("domain")
    x, h = lax.div(p, 2), lax.rem(p, 2)
    peer_x = [lax.rem(x + d, 4) for d in range(4)]
    peers = [(peer_x[d] * 2 + h, dom) for d in range(4)]
    partner = (x * 2 + 1 - h, dom)
    below, above = (p, lax.rem(dom + 31, 32)), (p, lax.rem(dom + 1, 32))

    def remote(src, dst, ss, rs, dev):
        return pltpu.make_async_remote_copy(
            src_ref=src, dst_ref=dst, send_sem=ss, recv_sem=rs, device_id=dev, device_id_type=MESH
        )

    lon = lambda k: pl.ds(k * WIDTH, WIDTH)
    chan = lambda g: pl.ds(g * GROUP, GROUP)

    def x1(k):
        return [
            remote(
                states.at[:, chan(peer_x[d]), :, lon(k)],
                mine[k].at[pl.ds(x * 4, 4)],
                s_x1.at[k, d - 1],
                r_x1.at[k, d - 1],
                peers[d],
            )
            for d in range(1, 4)
        ]

    own = [
        pltpu.make_async_copy(
            states.at[:, chan(x), :, lon(k)], mine[k].at[pl.ds(x * 4, 4)], l_x1.at[k]
        )
        for k in range(CHUNKS)
    ]
    pert_copy = pltpu.make_async_copy(pert, pert_v, l_c.at[0])
    pert_copy.start()
    for k in range(CHUNKS):
        own[k].start()

    lane = lax.broadcasted_iota(jnp.int32, (8, 128), 1)
    row = jnp.zeros((8, 128), jnp.int32)
    for i in range(4):
        row = jnp.where(lane == i, parents[i], row)
    par_send[...] = row
    par_x[pl.ds(x, 1)] = row[None]

    barrier = pltpu.get_barrier_semaphore()
    for dev in peers[1:] + [partner, below, above]:
        pl.semaphore_signal(barrier, inc=1, device_id=dev, device_id_type=MESH)
    pl.semaphore_wait(barrier, 6)

    sent = []

    def go(copies):
        for c in copies:
            c.start()
        sent.extend(copies)
        return copies

    par = go([remote(par_send, par_x.at[x], s_p.at[d - 1], r_p.at[d - 1], peers[d]) for d in range(1, 4)])
    first = {k: go(x1(k)) for k in range(AHEAD)}
    masks = go(
        [
            remote(mask, mask_halo.at[1], s_m.at[0], r_m.at[0], below),
            remote(mask, mask_halo.at[0], s_m.at[1], r_m.at[1], above),
        ]
    )
    for c in par:
        c.wait_recv()
    (par2,) = go([remote(par_x, par_z, s_q.at[0], r_q.at[0], partner)])
    to_smem = pltpu.make_async_copy(par_x, par_xs, l_c.at[1])
    to_smem.start()

    def set_bit(i, b):
        bits[i] = b
        return b + b

    lax.fori_loop(0, 32, set_bit, jnp.int32(1))
    to_smem.wait()
    par2.wait_recv()
    to_smem2 = pltpu.make_async_copy(par_z, par_zs, l_c.at[2])
    to_smem2.start()
    to_smem2.wait()

    def union(ref):
        return lax.fori_loop(
            0, HALF, lambda i, m: m | bits[ref[lax.div(i, 4), 0, lax.rem(i, 4)]], jnp.int32(0)
        )

    wanted_here, wanted_there = union(par_xs), union(par_zs)

    def scan(l, carry):
        n_out, n_in, out = carry
        base = lax.div(l, 4) * 8 + lax.rem(l, 4)
        here, there = base + h * 4, base + (1 - h) * 4
        out_bit = lax.shift_right_logical(wanted_there, here) & 1
        in_bit = lax.shift_right_logical(wanted_here, there) & 1
        table[here] = l
        table[there] = HALF + jnp.minimum(n_in, CAP - 1)
        out = tuple(
            jnp.where((out_bit == 1) & (n_out == c), l, old) for c, old in enumerate(out)
        )
        return n_out + out_bit, n_in + in_bit, out

    zero = jnp.int32(0)
    n_out, n_in, out = lax.fori_loop(0, HALF, scan, (zero, zero, (zero,) * CAP))
    for c in range(CAP):
        listed[c] = out[c]
    flag[0] = jnp.where((n_out > CAP) | (n_in > CAP), 1, 0).astype(jnp.int32)

    res4 = res.reshape(4, CH, ROWS, LON)
    strip4 = strip.reshape(4, CH, ROWS, WIDTH)
    z, second, halos = {}, {}, {}
    for t in range(CHUNKS + 2):
        if t < CHUNKS:
            k = t
            own[k].wait()
            for c in first[k]:
                c.wait_recv()

            def stage_z(c, carry, k=k):
                crossing[k][c] = mine[k][listed[c]]
                return carry

            lax.fori_loop(0, CAP, stage_z, 0)
            z[k] = go([remote(crossing[k], crossed[k], s_z.at[k], r_z.at[k], partner)])
            if k + AHEAD < CHUNKS:
                first[k + AHEAD] = go(x1(k + AHEAD))
        if 1 <= t <= CHUNKS:
            k = t - 1
            z[k][0].wait_recv()
            second[k] = []
            for d in (1, 2, 3, 0):

                def stage_x(j, carry, k=k, d=d):
                    s = table[par_xs[peer_x[d], 0, j]]
                    far = s >= HALF
                    a = mine[k][jnp.where(far, 0, s)]
                    b = crossed[k][jnp.where(far, s - HALF, 0)]
                    v = jnp.where(far, b, a)
                    if d == 0:
                        got[k][x, j] = v
                    else:
                        back[k][d - 1, j] = v
                    return carry

                lax.fori_loop(0, 4, stage_x, 0)
                if d:
                    second[k] += go(
                        [
                            remote(
                                back[k].at[d - 1],
                                got[k].at[x],
                                s_x2.at[k, d - 1],
                                r_x2.at[k, d - 1],
                                peers[d],
                            )
                        ]
                    )
        if t >= 2:
            k = t - 2
            if k == 0:
                pert_copy.wait()
            for c in second[k]:
                c.wait_recv()
            for g in range(4):
                new = got[k][g] + pert_v[:, chan(g), :, lon(k)]
                res4[:, chan(g), :, lon(k)] = new
                strip4[:, chan(g)] = new
            for i, r in enumerate((0, 1, 6, 7)):
                edge[k][i // 2, i % 2] = strip[pl.ds(r, 4 * CH, stride=ROWS)]
            halos[k] = go(
                [
                    remote(edge[k].at[0], halo.at[1, :, :, lon(k)], s_h.at[k, 0], r_h.at[k, 0], below),
                    remote(edge[k].at[1], halo.at[0, :, :, lon(k)], s_h.at[k, 1], r_h.at[k, 1], above),
                ]
            )
    for c in masks:
        c.wait_recv()
    for k in range(CHUNKS):
        for c in halos[k]:
            c.wait_recv()
    for c in sent:
        c.wait_send()


def routed(states, pert, parents, mask):
    dma = pltpu.SemaphoreType.DMA
    vm = lambda *s: pltpu.VMEM(s, jnp.float32)
    scratch = []
    for shape in (
        (HALF, GROUP, ROWS, WIDTH),
        (CAP, GROUP, ROWS, WIDTH),
        (CAP, GROUP, ROWS, WIDTH),
        (3, 4, GROUP, ROWS, WIDTH),
        (4, 4, GROUP, ROWS, WIDTH),
        (2, 2, 4 * CH, WIDTH),
    ):
        scratch += [vm(*shape)] * CHUNKS
    scratch += [
        vm(4, CH, ROWS, LON),
        vm(4 * CH * ROWS, WIDTH),
        pltpu.VMEM((8, 128), jnp.int32),
        pltpu.VMEM((4, 8, 128), jnp.int32),
        pltpu.VMEM((4, 8, 128), jnp.int32),
        pltpu.SMEM((4, 8, 128), jnp.int32),
        pltpu.SMEM((4, 8, 128), jnp.int32),
        pltpu.SMEM((32,), jnp.int32),
        pltpu.SMEM((32,), jnp.int32),
        pltpu.SMEM((CAP,), jnp.int32),
    ]
    three, two, one = dma((CHUNKS, 3)), dma((CHUNKS, 2)), dma((CHUNKS,))
    scratch += [three, three, one, one, one, three, three, two, two, dma((3,)), dma((3,)), dma((1,)), dma((1,)), dma((2,)), dma((2,)), dma((3,))]
    vmem = pl.BlockSpec(memory_space=pltpu.VMEM)
    smem = pl.BlockSpec(memory_space=pltpu.SMEM)
    hbm = pl.BlockSpec(memory_space=pl.ANY)
    return pl.pallas_call(
        route,
        name="route",
        out_shape=(
            jax.ShapeDtypeStruct((4 * CH * ROWS, LON), jnp.float32),
            jax.ShapeDtypeStruct((2, 2, 4 * CH, LON), jnp.float32),
            jax.ShapeDtypeStruct((2, ROWS, LON), jnp.int32),
            jax.ShapeDtypeStruct((1,), jnp.int32),
        ),
        in_specs=[hbm, hbm, smem, vmem],
        out_specs=(vmem, vmem, vmem, smem),
        scratch_shapes=scratch,
        compiler_params=pltpu.CompilerParams(
            collective_id=0, has_side_effects=True, vmem_limit_bytes=48 << 20
        ),
    )(states, pert, parents, mask)


INNER = CH * ROWS
MIDDLE = INNER + 2 * WIN
OUTER = INNER + 4 * WIN


def place(i, off):
    q = i - INNER
    window = (q >= WIN).astype(jnp.int32) + (q >= 2 * WIN) + (q >= 3 * WIN)
    inside = i < INNER
    ch = jnp.where(inside, i >> 3, q - window * WIN - off)
    outer_row = jnp.where(window == 0, -1, jnp.where(window == 1, 8, jnp.where(window == 2, -2, 9)))
    return ch, jnp.where(inside, i & 7, outer_row)


def stencil(coupling, diffusivity, rows, cols, off):
    high = functools.partial(jnp.dot, preferred_element_type=jnp.float32, precision=lax.Precision.HIGHEST)
    ch_a, _ = place(lax.broadcasted_iota(jnp.int32, (rows, CH), 0), off)
    pick_a = (ch_a == lax.broadcasted_iota(jnp.int32, (rows, CH), 1)).astype(jnp.float32)
    ch_b, _ = place(lax.broadcasted_iota(jnp.int32, (CH, cols), 1), off)
    pick_b = (ch_b == lax.broadcasted_iota(jnp.int32, (CH, cols), 0)).astype(jnp.float32)
    full = high(high(pick_a, coupling), pick_b)
    d = jnp.sum(pick_a * diffusivity, axis=1, keepdims=True)
    shape = (rows, cols)
    ci, ri = place(lax.broadcasted_iota(jnp.int32, shape, 0), off)
    cj, rj = place(lax.broadcasted_iota(jnp.int32, shape, 1), off)
    real = (ci >= 0) & (ci < CH) & (cj >= 0) & (cj < CH)
    gap = ri - rj
    vertical = jnp.where(gap == 0, -4.0, jnp.where((gap == 1) | (gap == -1), 1.0, 0.0))
    m = jnp.where(gap == 0, full, 0.0) + jnp.where(ci == cj, vertical * d, 0.0)
    return jnp.where(real, m, 0.0), d


def halves(v):
    top = v.astype(jnp.bfloat16)
    return top, (v - top.astype(jnp.float32)).astype(jnp.bfloat16)


def apply(mat, v):
    dot = functools.partial(jnp.dot, preferred_element_type=jnp.float32)
    top, low = halves(v)
    n = mat.shape[0] // 2
    both = dot(mat[...], top)
    return both[:n] + both[n:] + dot(mat[:n], low)


def sides(v):
    return pltpu.roll(v, 1, 1) + pltpu.roll(v, LON - 1, 1)


def model(res, halo, mask, mask_halo, coupling, diffusivity, out, mat1, mat2, diff, land):
    j = pl.program_id(0)
    dom = lax.axis_index("domain")
    has_low = (dom > 0).astype(jnp.float32)
    has_high = (dom < 31).astype(jnp.float32)

    @pl.when(j == 0)
    def _():
        for odd in range(2):
            m, d = stencil(coupling[...], diffusivity[...], MIDDLE, OUTER, 4 * odd)
            top, low = halves(m)
            mat1[odd, :MIDDLE] = top
            mat1[odd, MIDDLE:] = low
            diff[odd] = jnp.broadcast_to(d, (MIDDLE, 128))
            m, _ = stencil(coupling[...], diffusivity[...], INNER, MIDDLE, 4 * odd)
            top, low = halves(m)
            mat2[odd, :INNER] = top
            mat2[odd, INNER:] = low
        sea = mask[...].astype(jnp.float32)
        for c in range(CH):
            land[pl.ds(c * ROWS, ROWS)] = sea
        low = mask_halo[0, ROWS - 1 : ROWS].astype(jnp.float32) * has_low
        high = mask_halo[1, 0:1].astype(jnp.float32) * has_high
        land[pl.ds(INNER, WIN)] = jnp.broadcast_to(low, (WIN, LON))
        land[pl.ds(INNER + WIN, WIN)] = jnp.broadcast_to(high, (WIN, LON))

    odd = lax.rem(j, 2)
    start = pl.multiple_of(lax.div(j, 2) * 40 + odd * 16, 8)
    rows = pl.ds(start, WIN)
    v = jnp.concatenate(
        [
            res[0],
            halo[0, 1, rows] * has_low,
            halo[1, 0, rows] * has_high,
            halo[0, 0, rows] * has_low,
            halo[1, 1, rows] * has_high,
        ],
        axis=0,
    )
    d = diff[odd][:, :1]
    u = v[:MIDDLE]
    first = u + land[...] * (apply(mat1.at[odd], v) + d * sides(u))
    inner = first[:INNER]
    out[0] = inner + land[:INNER] * (apply(mat2.at[odd], first) + d[:INNER] * sides(inner))


def modelled(res, halo, mask, mask_halo, coupling, diffusivity):
    whole = pl.BlockSpec(memory_space=pltpu.VMEM)
    block = pl.BlockSpec((1, INNER, LON), lambda j: (j, 0, 0))
    return pl.pallas_call(
        model,
        name="model",
        grid=(4,),
        out_shape=jax.ShapeDtypeStruct((4, INNER, LON), jnp.float32),
        in_specs=[block, whole, whole, whole, whole, whole],
        out_specs=block,
        scratch_shapes=[
            pltpu.VMEM((2, 2 * MIDDLE, OUTER), jnp.bfloat16),
            pltpu.VMEM((2, 2 * INNER, MIDDLE), jnp.bfloat16),
            pltpu.VMEM((2, MIDDLE, 128), jnp.float32),
            pltpu.VMEM((MIDDLE, LON), jnp.float32),
        ],
        compiler_params=pltpu.CompilerParams(vmem_limit_bytes=48 << 20),
    )(res, halo, mask, mask_halo, coupling, diffusivity)


def with_halo(block):
    count = lax.axis_size("domain")
    forward = [(i, i + 1) for i in range(count - 1)]
    backward = [(target, source) for source, target in forward]
    low = lax.ppermute(block[:, :, -1:], "domain", forward)
    high = lax.ppermute(block[:, :, :1], "domain", backward)
    return jnp.concatenate([low, block, high], axis=2)


def advance(padded, mask_rows, diffusivity, coupling):
    center = padded[:, :, 1:-1]
    laplace = (
        padded[:, :, :-2]
        + padded[:, :, 2:]
        + jnp.roll(center, 1, 3)
        + jnp.roll(center, -1, 3)
        - 4.0 * center
    )
    coupled = jnp.einsum("cd,pdrl->pcrl", coupling, center, precision=lax.Precision.HIGHEST)
    return center + mask_rows[None, None] * (diffusivity[None, :, None, None] * laplace + coupled)


def gathered(states, parents, perturbation, sea_mask, diffusivity, coupling):
    shard_rows = lax.all_gather(states, "particle", axis=0, tiled=True)
    fields = jnp.take(shard_rows, parents, axis=0) + perturbation
    mask_rows = sea_mask.astype(jnp.float32)
    for _ in range(2):
        fields = advance(with_halo(fields), mask_rows, diffusivity, coupling)
    return fields


def on_device(states, parents, perturbation, sea_mask, diffusivity, coupling):
    res, halo, mask_halo, flag = routed(states, perturbation, parents, sea_mask)

    def usual():
        out = modelled(
            res.reshape(4, INNER, LON), halo, sea_mask, mask_halo, coupling, diffusivity[None]
        )
        return out.reshape(4, CH, ROWS, LON)

    def crowded():
        return gathered(states, parents, perturbation, sea_mask, diffusivity, coupling)

    return lax.cond(flag[0] > 0, crowded, usual)


def solution(mesh):
    in_specs = (
        P("particle", None, "domain", None),
        P("particle"),
        P("particle", None, "domain", None),
        P("domain", None),
        P(),
        P(),
    )
    out_specs = P("particle", None, "domain", None)
    return jax.shard_map(
        on_device, mesh=mesh, in_specs=in_specs, out_specs=out_specs, check_vma=False
    )
```

time: 463 us -> 115 us (0.25)
  waiting for transfers between devices: 384 us -> 0 us
  Pallas kernels: 0 us -> 98 us
  matrix products: 38.4 us -> 0 us
  starting transfers between devices: 10.1 us -> 0 us
  other arithmetic: 8.74 us -> 0 us
  local copies, waits for them, and re-layouts: 7.74 us -> 1.5 us
    all_gather x1 -> x0, waiting for transfers between devices: 379 us -> none  [on_device(): shard_rows = lax.all_gather(states, 'particle', axis=0, tiled=True)]
    pallas_call x0 -> x2, Pallas kernels: none -> 98 us  [the longest x1 91.6 us: routed(): pl.pallas_call(route, name='route', out_shape=(jax.ShapeDtypeStruct((4 *...]
    dot_general x3 -> x0, matrix products: 38.4 us -> none  [the longest x1 27.1 us: on_device(): jnp.einsum('ji,icrl->jcrl', chosen, shard_rows, precision=lax.Precision.H...]
    ppermute x4 -> x0, starting transfers between devices: 10 us -> none  [the longest x2 5.15 us: with_halo(): lax.ppermute(lax.slice_in_dim(block, 0, width, axis=dim), axis, backward)]
    add x2 -> x0, other arithmetic: 8.74 us -> none  [advance(): center + mask_rows[None, None] * (diffusivity[None, :, None, None] * lapl...]
    slice x6 -> x0, local copies, waits for them, and re-layouts: 4.67 us -> none  [the longest x4 4.57 us: advance(): jnp.roll(center, -1, 3)]
  transfers between devices with their start and end apart: 5 -> 0, of which waited for: 3 -> 0; matrix products, arithmetic and copies ran while one was open for 2% -> 0% of each run, Pallas kernels for 0% -> 0%
where the time goes in v1:
time: 115 us; the launch traced here: 114 us
  Pallas kernels  98 us (85%)
  between operations  14.1 us (12%)
  local copies, waits for them, and re-layouts  1.5 us (1%)
    pallas_call x1, Pallas kernels, routed(): pl.pallas_call(route, name='route', out_shape=(jax.ShapeDtypeStruct((4 *...  91.6 us
    pallas_call x1, Pallas kernels, modelled(): pl.pallas_call(model, name='model', grid=(4,), out_shape=jax.ShapeDtypeSt...  6.4 us

profile of v1, /device:TPU:25, one launch (start us, length us, event | category | flops | bytes accessed | tf_op | source)
XLA Modules:
  0.0 113.8 jit_solution(806119478768677861)
XLA Ops:
  6.5 0.0 copy-start
  6.5 0.0 copy-start.2
  6.5 0.0 copy-start.5
  6.5 0.0 copy-start.4
  6.5 0.0 copy-start.3
  6.5 91.6 %route.1 = (f32[640,1024]{1,0:T(8,128)S(1)}, f32[2,2,80,1024]{3,2,1,0:T(8,128)S(1)}, s32[2,8,1024]{2,1,0:T(8,128)S(1)}, s32[1]{0:T(128)}) custom-call(f32[4,20,8,1024]{3,2,1,0:T(8,128)} %states.1, f32[4,20,8,1024]{3,2,1,0:T(8,128)} %pert.1, s32[4]{0:T(128)} %parents.1, s32[8,1024]{1,0:T(8,128)} %mask.1), custom_call_target="tpu_custom_call" | custom-call | tf_op jit(solution)/shard_map/route/pallas_call | solution.py:244
  98.7 0.0 copy-done
  98.8 0.0 copy-done.2
  98.8 0.0 copy-done.5
  98.8 0.0 copy-done.4
  98.8 0.0 copy-done.3
  98.8 6.6 %conditional.1 = (f32[4,20,8,1024]{3,2,1,0:T(8,128)S(1)}) conditional(s32[]{:T(128)} %bitcast.8, (f32[640,1024]{1,0:T(8,128)S(1)}, f32[20]{0:T(128)S(1)}, f32[2,2,80,1024]{3,2,1,0:T(8,128)S(1)}, s32[8,1024]{1,0:T(8,128)S(1)}, s32[2,8,1024]{2,1,0:T(8,128)S(1)}, /*index=5*/f32[20,20]{1,0:T(8,128)S(1)}) %tuple.39, (s32[4]{0:T(128)S(1)}, ...), branch_computations={%region_0.0_spmd, %region_1.2_spmd} | conditional | flops 332932128 | bytes 140385856 | solution.py:420
  98.8 6.4 %model.1 = f32[4,160,1024]{2,1,0:T(8,128)S(1)} custom-call(f32[4,160,1024]{2,1,0:T(8,128)S(1)} %bitcast.17, f32[2,2,80,1024]{3,2,1,0:T(8,128)S(1)} %get-tuple-element.33.halo, s32[8,1024]{1,0:T(8,128)S(1)} %get-tuple-element.34.mask, s32[2,8,1024]{2,1,0:T(8,128)S(1)} %get-tuple-element.35.mask_halo, f32[20,20]{1,0:T(8,128)S(1)} %get-tuple-element.36.coupling, ...), custom_call_target="tpu_custom_call" | custom-call | tf_op jit(solution)/shard_map/cond/branch_0_fun/model/pallas_call | solution.py:360
  105.4 0.0 copy-start.1
  105.5 1.5 %copy-done.1 = f32[4,20,8,1024]{3,2,1,0:T(8,128)} copy-done((f32[4,20,8,1024]{3,2,1,0:T(8,128)}, f32[4,20,8,1024]{3,2,1,0:T(8,128)S(1)}, u32[]{:S(2)}) %copy-start.1) | copy-done | bytes 2621464
Async XLA Ops:
  6.5 92.2 %copy-start = (f32[4,20,8,1024]{3,2,1,0:T(8,128)S(1)}, f32[4,20,8,1024]{3,2,1,0:T(8,128)}, u32[]{:S(2)}) copy-start(f32[4,20,8,1024]{3,2,1,0:T(8,128)} %pert.1) | copy-start | bytes 7864324
  6.5 92.2 %copy-start.2 = (s32[8,1024]{1,0:T(8,128)S(1)}, s32[8,1024]{1,0:T(8,128)}, u32[]{:S(2)}) copy-start(s32[8,1024]{1,0:T(8,128)} %mask.1) | copy-start | bytes 98308
  6.5 92.2 %copy-start.5 = (s32[4]{0:T(128)S(1)}, s32[4]{0:T(128)}, u32[]{:S(2)}) copy-start(s32[4]{0:T(128)} %parents.1) | copy-start | bytes 52
  6.5 92.2 %copy-start.4 = (f32[20]{0:T(128)S(1)}, f32[20]{0:T(128)}, u32[]{:S(2)}) copy-start(f32[20]{0:T(128)} %param.12) | copy-start | bytes 244
  6.5 92.2 %copy-start.3 = (f32[20,20]{1,0:T(8,128)S(1)}, f32[20,20]{1,0:T(8,128)}, u32[]{:S(2)}) copy-start(f32[20,20]{1,0:T(8,128)} %param.13) | copy-start | bytes 4804
  105.4 1.5 %copy-start.1 = (f32[4,20,8,1024]{3,2,1,0:T(8,128)}, f32[4,20,8,1024]{3,2,1,0:T(8,128)S(1)}, u32[]{:S(2)}) copy-start(f32[4,20,8,1024]{3,2,1,0:T(8,128)S(1)} %get-tuple-element.92) | copy-start | bytes 7864324

commit v2 on v1

--- a/solution.py
+++ b/solution.py
@@ -14,14 +14,20 @@
 CHUNKS = 8
 WIDTH = LON // CHUNKS
 AHEAD = 3
+LZ, LX = 2, 1
+UNITS = [(k, 0, GROUP) for k in range(CHUNKS)]
+N_UNITS = len(UNITS)
 WIN = 24
 
 
-def route(states, pert, parents, mask, res, halo, mask_halo, flag, *scratch):
+def route(
+    states, pert, parents, mask, coupling, diffusivity,
+    res, halo, mask_halo, flag, mat1, mat2, diff, land, *scratch
+):
     it = iter(scratch)
-    take = lambda: [next(it) for _ in range(CHUNKS)]
-    mine, crossing, crossed, back, got = take(), take(), take(), take(), take()
-    edge = take()
+    take = lambda n: [next(it) for _ in range(n)]
+    mine, crossing, crossed, back, got = (take(N_UNITS) for _ in range(5))
+    edge = take(CHUNKS)
     (pert_v, strip, par_send, par_x, par_z, par_xs, par_zs, bits, table, listed) = (next(it) for _ in range(10))
     (s_x1, r_x1, l_x1, s_z, r_z, s_x2, r_x2, s_h, r_h, s_p, r_p, s_q, r_q, s_m, r_m, l_c) = (
         next(it) for _ in range(16)
@@ -39,12 +45,12 @@
         )
 
     lon = lambda k: pl.ds(k * WIDTH, WIDTH)
-    chan = lambda g: pl.ds(g * GROUP, GROUP)
+    chan = lambda g, u: pl.ds(g * GROUP + UNITS[u][1], UNITS[u][2])
 
     def x1(k):
         return [
             remote(
-                states.at[:, chan(peer_x[d]), :, lon(k)],
+                states.at[:, chan(peer_x[d], k), :, lon(UNITS[k][0])],
                 mine[k].at[pl.ds(x * 4, 4)],
                 s_x1.at[k, d - 1],
                 r_x1.at[k, d - 1],
@@ -55,13 +61,13 @@
 
     own = [
         pltpu.make_async_copy(
-            states.at[:, chan(x), :, lon(k)], mine[k].at[pl.ds(x * 4, 4)], l_x1.at[k]
+            states.at[:, chan(x, k), :, lon(UNITS[k][0])], mine[k].at[pl.ds(x * 4, 4)], l_x1.at[k]
         )
-        for k in range(CHUNKS)
+        for k in range(N_UNITS)
     ]
     pert_copy = pltpu.make_async_copy(pert, pert_v, l_c.at[0])
     pert_copy.start()
-    for k in range(CHUNKS):
+    for k in range(N_UNITS):
         own[k].start()
 
     lane = lax.broadcasted_iota(jnp.int32, (8, 128), 1)
@@ -86,12 +92,23 @@
 
     par = go([remote(par_send, par_x.at[x], s_p.at[d - 1], r_p.at[d - 1], peers[d]) for d in range(1, 4)])
     first = {k: go(x1(k)) for k in range(AHEAD)}
-    masks = go(
-        [
-            remote(mask, mask_halo.at[1], s_m.at[0], r_m.at[0], below),
-            remote(mask, mask_halo.at[0], s_m.at[1], r_m.at[1], above),
-        ]
-    )
+    masks = [
+        remote(mask, mask_halo.at[1], s_m.at[0], r_m.at[0], below),
+        remote(mask, mask_halo.at[0], s_m.at[1], r_m.at[1], above),
+    ]
+    pl.when(dom > 0)(masks[0].start)
+    pl.when(dom < 31)(masks[1].start)
+
+    @pl.when(dom == 0)
+    def _():
+        halo[0] = jnp.zeros(halo.shape[1:], jnp.float32)
+        mask_halo[0] = jnp.zeros(mask_halo.shape[1:], jnp.int32)
+
+    @pl.when(dom == 31)
+    def _():
+        halo[1] = jnp.zeros(halo.shape[1:], jnp.float32)
+        mask_halo[1] = jnp.zeros(mask_halo.shape[1:], jnp.int32)
+
     for c in par:
         c.wait_recv()
     (par2,) = go([remote(par_x, par_z, s_q.at[0], r_q.at[0], partner)])
@@ -104,42 +121,56 @@
 
     lax.fori_loop(0, 32, set_bit, jnp.int32(1))
     to_smem.wait()
+
+    def union(ref):
+        return lax.fori_loop(
+            0, HALF, lambda i, m: m | bits[ref[lax.div(i, 4), 0, lax.rem(i, 4)]], jnp.int32(0), unroll=4
+        )
+
+    def member(l, half):
+        return lax.div(l, 4) * 8 + half * 4 + lax.rem(l, 4)
+
+    for odd in range(2):
+        build(coupling[...], diffusivity[...], odd, mat1, mat2, diff)
+    wanted_here = union(par_xs)
+
+    def arrivals(l, count):
+        here, there = member(l, h), member(l, 1 - h)
+        table[here] = l
+        table[there] = HALF + jnp.minimum(count, CAP - 1)
+        return count + (lax.shift_right_logical(wanted_here, there) & 1)
+
+    zero = jnp.int32(0)
+    n_in = lax.fori_loop(0, HALF, arrivals, zero, unroll=4)
     par2.wait_recv()
     to_smem2 = pltpu.make_async_copy(par_z, par_zs, l_c.at[2])
     to_smem2.start()
     to_smem2.wait()
-
-    def union(ref):
-        return lax.fori_loop(
-            0, HALF, lambda i, m: m | bits[ref[lax.div(i, 4), 0, lax.rem(i, 4)]], jnp.int32(0)
+    wanted_there = union(par_zs)
+
+    def departures(l, carry):
+        count, out = carry
+        bit = lax.shift_right_logical(wanted_there, member(l, h)) & 1
+        out = tuple(
+            jnp.where((bit == 1) & (count == c), l, old) for c, old in enumerate(out)
         )
-
-    wanted_here, wanted_there = union(par_xs), union(par_zs)
-
-    def scan(l, carry):
-        n_out, n_in, out = carry
-        base = lax.div(l, 4) * 8 + lax.rem(l, 4)
-        here, there = base + h * 4, base + (1 - h) * 4
-        out_bit = lax.shift_right_logical(wanted_there, here) & 1
-        in_bit = lax.shift_right_logical(wanted_here, there) & 1
-        table[here] = l
-        table[there] = HALF + jnp.minimum(n_in, CAP - 1)
-        out = tuple(
-            jnp.where((out_bit == 1) & (n_out == c), l, old) for c, old in enumerate(out)
-        )
-        return n_out + out_bit, n_in + in_bit, out
-
-    zero = jnp.int32(0)
-    n_out, n_in, out = lax.fori_loop(0, HALF, scan, (zero, zero, (zero,) * CAP))
+        return count + bit, out
+
+    n_out, out = lax.fori_loop(0, HALF, departures, (zero, (zero,) * CAP), unroll=4)
     for c in range(CAP):
         listed[c] = out[c]
     flag[0] = jnp.where((n_out > CAP) | (n_in > CAP), 1, 0).astype(jnp.int32)
 
+    def wait_rows(copies):
+        down, up = copies
+        pl.when(dom < 31)(down.wait_recv)
+        pl.when(dom > 0)(up.wait_recv)
+
     res4 = res.reshape(4, CH, ROWS, LON)
     strip4 = strip.reshape(4, CH, ROWS, WIDTH)
     z, second, halos = {}, {}, {}
-    for t in range(CHUNKS + 2):
-        if t < CHUNKS:
+    for t in range(N_UNITS + LZ + LX):
+        if t < N_UNITS:
             k = t
             own[k].wait()
             for c in first[k]:
@@ -151,10 +182,19 @@
 
             lax.fori_loop(0, CAP, stage_z, 0)
             z[k] = go([remote(crossing[k], crossed[k], s_z.at[k], r_z.at[k], partner)])
-            if k + AHEAD < CHUNKS:
+            if k + AHEAD < N_UNITS:
                 first[k + AHEAD] = go(x1(k + AHEAD))
-        if 1 <= t <= CHUNKS:
-            k = t - 1
+        if t == 2:
+            wait_rows(masks)
+            sea = mask[...].astype(jnp.float32)
+            for c in range(CH):
+                land[pl.ds(c * ROWS, ROWS)] = sea
+            low = mask_halo[0, ROWS - 1 : ROWS].astype(jnp.float32)
+            high = mask_halo[1, 0:1].astype(jnp.float32)
+            land[pl.ds(INNER, WIN)] = jnp.broadcast_to(low, (WIN, LON))
+            land[pl.ds(INNER + WIN, WIN)] = jnp.broadcast_to(high, (WIN, LON))
+        if LZ <= t < N_UNITS + LZ:
+            k = t - LZ
             z[k][0].wait_recv()
             second[k] = []
             for d in (1, 2, 3, 0):
@@ -184,46 +224,43 @@
                             )
                         ]
                     )
-        if t >= 2:
-            k = t - 2
+        if t >= LZ + LX:
+            k = t - LZ - LX
             if k == 0:
                 pert_copy.wait()
             for c in second[k]:
                 c.wait_recv()
+            u, (k, _, _) = k, UNITS[k]
             for g in range(4):
-                new = got[k][g] + pert_v[:, chan(g), :, lon(k)]
-                res4[:, chan(g), :, lon(k)] = new
-                strip4[:, chan(g)] = new
+                new = got[u][g] + pert_v[:, chan(g, u), :, lon(k)]
+                res4[:, chan(g, u), :, lon(k)] = new
+                strip4[:, chan(g, u)] = new
+            if u + 1 < N_UNITS and UNITS[u + 1][0] == k:
+                continue
             for i, r in enumerate((0, 1, 6, 7)):
                 edge[k][i // 2, i % 2] = strip[pl.ds(r, 4 * CH, stride=ROWS)]
-            halos[k] = go(
-                [
-                    remote(edge[k].at[0], halo.at[1, :, :, lon(k)], s_h.at[k, 0], r_h.at[k, 0], below),
-                    remote(edge[k].at[1], halo.at[0, :, :, lon(k)], s_h.at[k, 1], r_h.at[k, 1], above),
-                ]
-            )
-    for c in masks:
-        c.wait_recv()
+            halos[k] = [
+                remote(edge[k].at[0], halo.at[1, :, :, lon(k)], s_h.at[k, 0], r_h.at[k, 0], below),
+                remote(edge[k].at[1], halo.at[0, :, :, lon(k)], s_h.at[k, 1], r_h.at[k, 1], above),
+            ]
+            pl.when(dom > 0)(halos[k][0].start)
+            pl.when(dom < 31)(halos[k][1].start)
     for k in range(CHUNKS):
-        for c in halos[k]:
-            c.wait_recv()
+        wait_rows(halos[k])
     for c in sent:
         c.wait_send()
-
-
-def routed(states, pert, parents, mask):
+    for down, up in [masks] + [halos[k] for k in range(CHUNKS)]:
+        pl.when(dom > 0)(down.wait_send)
+        pl.when(dom < 31)(up.wait_send)
+
+
+def routed(states, pert, parents, mask, coupling, diffusivity):
     dma = pltpu.SemaphoreType.DMA
     vm = lambda *s: pltpu.VMEM(s, jnp.float32)
     scratch = []
-    for shape in (
-        (HALF, GROUP, ROWS, WIDTH),
-        (CAP, GROUP, ROWS, WIDTH),
-        (CAP, GROUP, ROWS, WIDTH),
-        (3, 4, GROUP, ROWS, WIDTH),
-        (4, 4, GROUP, ROWS, WIDTH),
-        (2, 2, 4 * CH, WIDTH),
-    ):
-        scratch += [vm(*shape)] * CHUNKS
+    for lead in ((HALF,), (CAP,), (CAP,), (3, 4), (4, 4)):
+        scratch += [vm(*lead, unit[2], ROWS, WIDTH) for unit in UNITS]
+    scratch += [vm(2, 2, 4 * CH, WIDTH)] * CHUNKS
     scratch += [
         vm(4, CH, ROWS, LON),
         vm(4 * CH * ROWS, WIDTH),
@@ -236,7 +273,7 @@
         pltpu.SMEM((32,), jnp.int32),
         pltpu.SMEM((CAP,), jnp.int32),
     ]
-    three, two, one = dma((CHUNKS, 3)), dma((CHUNKS, 2)), dma((CHUNKS,))
+    three, two, one = dma((N_UNITS, 3)), dma((CHUNKS, 2)), dma((N_UNITS,))
     scratch += [three, three, one, one, one, three, three, two, two, dma((3,)), dma((3,)), dma((1,)), dma((1,)), dma((2,)), dma((2,)), dma((3,))]
     vmem = pl.BlockSpec(memory_space=pltpu.VMEM)
     smem = pl.BlockSpec(memory_space=pltpu.SMEM)
@@ -249,14 +286,18 @@
             jax.ShapeDtypeStruct((2, 2, 4 * CH, LON), jnp.float32),
             jax.ShapeDtypeStruct((2, ROWS, LON), jnp.int32),
             jax.ShapeDtypeStruct((1,), jnp.int32),
+            jax.ShapeDtypeStruct((2, 2 * MIDDLE, OUTER), jnp.bfloat16),
+            jax.ShapeDtypeStruct((2, 2 * INNER, MIDDLE), jnp.bfloat16),
+            jax.ShapeDtypeStruct((2, MIDDLE, 128), jnp.float32),
+            jax.ShapeDtypeStruct((MIDDLE, LON), jnp.float32),
         ),
-        in_specs=[hbm, hbm, smem, vmem],
-        out_specs=(vmem, vmem, vmem, smem),
+        in_specs=[hbm, hbm, smem, vmem, vmem, vmem],
+        out_specs=(vmem, vmem, vmem, smem, vmem, vmem, vmem, vmem),
         scratch_shapes=scratch,
         compiler_params=pltpu.CompilerParams(
             collective_id=0, has_side_effects=True, vmem_limit_bytes=48 << 20
         ),
-    )(states, pert, parents, mask)
+    )(states, pert, parents, mask, coupling, diffusivity)
 
 
 INNER = CH * ROWS
@@ -304,35 +345,24 @@
     return both[:n] + both[n:] + dot(mat[:n], low)
 
 
+def build(coupling, diffusivity, odd, mat1, mat2, diff):
+    m, d = stencil(coupling, diffusivity, MIDDLE, OUTER, 4 * odd)
+    top, low = halves(m)
+    mat1[odd, :MIDDLE] = top
+    mat1[odd, MIDDLE:] = low
+    diff[odd] = jnp.broadcast_to(d, (MIDDLE, 128))
+    m, _ = stencil(coupling, diffusivity, INNER, MIDDLE, 4 * odd)
+    top, low = halves(m)
+    mat2[odd, :INNER] = top
+    mat2[odd, INNER:] = low
+
+
 def sides(v):
     return pltpu.roll(v, 1, 1) + pltpu.roll(v, LON - 1, 1)
 
 
-def model(res, halo, mask, mask_halo, coupling, diffusivity, out, mat1, mat2, diff, land):
+def model(res, halo, mat1, mat2, diff, land, out):
     j = pl.program_id(0)
-    dom = lax.axis_index("domain")
-    has_low = (dom > 0).astype(jnp.float32)
-    has_high = (dom < 31).astype(jnp.float32)
-
-    @pl.when(j == 0)
-    def _():
-        for odd in range(2):
-            m, d = stencil(coupling[...], diffusivity[...], MIDDLE, OUTER, 4 * odd)
-            top, low = halves(m)
-            mat1[odd, :MIDDLE] = top
-            mat1[odd, MIDDLE:] = low
-            diff[odd] = jnp.broadcast_to(d, (MIDDLE, 128))
-            m, _ = stencil(coupling[...], diffusivity[...], INNER, MIDDLE, 4 * odd)
-            top, low = halves(m)
-            mat2[odd, :INNER] = top
-            mat2[odd, INNER:] = low
-        sea = mask[...].astype(jnp.float32)
-        for c in range(CH):
-            land[pl.ds(c * ROWS, ROWS)] = sea
-        low = mask_halo[0, ROWS - 1 : ROWS].astype(jnp.float32) * has_low
-        high = mask_halo[1, 0:1].astype(jnp.float32) * has_high
-        land[pl.ds(INNER, WIN)] = jnp.broadcast_to(low, (WIN, LON))
-        land[pl.ds(INNER + WIN, WIN)] = jnp.broadcast_to(high, (WIN, LON))
 
     odd = lax.rem(j, 2)
     start = pl.multiple_of(lax.div(j, 2) * 40 + odd * 16, 8)
@@ -340,10 +370,10 @@
     v = jnp.concatenate(
         [
             res[0],
-            halo[0, 1, rows] * has_low,
-            halo[1, 0, rows] * has_high,
-            halo[0, 0, rows] * has_low,
-            halo[1, 1, rows] * has_high,
+            halo[0, 1, rows],
+            halo[1, 0, rows],
+            halo[0, 0, rows],
+            halo[1, 1, rows],
         ],
         axis=0,
     )
@@ -354,24 +384,18 @@
     out[0] = inner + land[:INNER] * (apply(mat2.at[odd], first) + d[:INNER] * sides(inner))
 
 
-def modelled(res, halo, mask, mask_halo, coupling, diffusivity):
+def modelled(res, halo, mat1, mat2, diff, land):
     whole = pl.BlockSpec(memory_space=pltpu.VMEM)
     block = pl.BlockSpec((1, INNER, LON), lambda j: (j, 0, 0))
     return pl.pallas_call(
         model,
         name="model",
         grid=(4,),
-        out_shape=jax.ShapeDtypeStruct((4, INNER, LON), jnp.float32),
+        out_shape=pltpu.HBM((4, INNER, LON), jnp.float32),
         in_specs=[block, whole, whole, whole, whole, whole],
         out_specs=block,
-        scratch_shapes=[
-            pltpu.VMEM((2, 2 * MIDDLE, OUTER), jnp.bfloat16),
-            pltpu.VMEM((2, 2 * INNER, MIDDLE), jnp.bfloat16),
-            pltpu.VMEM((2, MIDDLE, 128), jnp.float32),
-            pltpu.VMEM((MIDDLE, LON), jnp.float32),
-        ],
         compiler_params=pltpu.CompilerParams(vmem_limit_bytes=48 << 20),
-    )(res, halo, mask, mask_halo, coupling, diffusivity)
+    )(res, halo, mat1, mat2, diff, land)
 
 
 def with_halo(block):
@@ -406,13 +430,12 @@
 
 
 def on_device(states, parents, perturbation, sea_mask, diffusivity, coupling):
-    res, halo, mask_halo, flag = routed(states, perturbation, parents, sea_mask)
+    res, halo, _, flag, *fixed = routed(
+        states, perturbation, parents, sea_mask, coupling, diffusivity[None]
+    )
 
     def usual():
-        out = modelled(
-            res.reshape(4, INNER, LON), halo, sea_mask, mask_halo, coupling, diffusivity[None]
-        )
-        return out.reshape(4, CH, ROWS, LON)
+        return modelled(res.reshape(4, INNER, LON), halo, *fixed).reshape(4, CH, ROWS, LON)
 
     def crowded():
         return gathered(states, parents, perturbation, sea_mask, diffusivity, coupling)

time: 115 us -> 110 us (0.957)
  Pallas kernels: 98 us -> 94.8 us
  local copies, waits for them, and re-layouts: 1.5 us -> 0.02 us
    pallas_call x1, Pallas kernels: 91.6 us -> 89.1 us  [routed(): pl.pallas_call(route, name='route', out_shape=(jax.ShapeDtypeStruct((4 *...]
    unnamed x12 -> x10, local copies, waits for them, and re-layouts: 1.5 us -> 0.02 us
where the time goes in v2:
time: 110 us; the launch traced here: 109 us
  Pallas kernels  94.8 us (86%)
  between operations  14.1 us (13%)
    pallas_call x1, Pallas kernels, routed(): pl.pallas_call(route, name='route', out_shape=(jax.ShapeDtypeStruct((4 *...  89.1 us
    pallas_call x1, Pallas kernels, modelled(): pl.pallas_call(model, name='model', grid=(4,), out_shape=pltpu.HBM((4, IN...  5.69 us

profile of v2, /device:TPU:25, one launch (start us, length us, event | category | flops | bytes accessed | tf_op | source)
XLA Modules:
  0.0 109.0 jit_solution(15370517828052242186)
XLA Ops:
  6.5 0.0 copy-start.4
  6.5 0.0 copy-start
  6.5 0.0 copy-start.1
  6.5 0.0 copy-start.2
  6.5 0.0 copy-start.3
  6.5 89.1 %route.1 = (f32[640,1024]{1,0:T(8,128)S(1)}, f32[2,2,80,1024]{3,2,1,0:T(8,128)S(1)}, s32[2,8,1024]{2,1,0:T(8,128)}, s32[1]{0:T(128)}, bf16[2,416,256]{2,1,0:T(8,...) custom-call(f32[4,20,8,1024]{3,2,1,0:T(8,128)} %states.1, ...), custom_call_target="tpu_custom_call" | custom-call | tf_op jit(solution)/shard_map/route/pallas_call | solution.py:281
  96.4 0.0 copy-done.4
  96.4 0.0 copy-done
  96.4 0.0 copy-done.1
  96.4 0.0 copy-done.2
  96.4 0.0 copy-done.3
  96.4 5.7 %conditional.1 = (f32[4,20,8,1024]{3,2,1,0:T(8,128)}) conditional(s32[]{:T(128)} %bitcast.8, (f32[640,1024]{1,0:T(8,128)S(1)}, f32[2,2,80,1024]{3,2,1,0:T(8,128)S(1)}, bf16[2,416,256]{2,1,0:T(8,128)(2,1)S(1)}, bf16[2,320,208]{2,1,0:T(8,128)(2,1)S(1)}, f32[2,208,128]{2,1,0:T(8,128)S(1)}, /*index=5*/f32[208,1024]{1,0:T(8,128)S(1)}) %tuple.11, ...), branch_computations={%region_0.0_spmd, %region_1.2_spmd} | conditional | flops 332932128 | bytes 140385856 | solution.py:443
  96.5 5.7 %model.1 = f32[4,160,1024]{2,1,0:T(8,128)} custom-call(f32[4,160,1024]{2,1,0:T(8,128)S(1)} %bitcast.17, f32[2,2,80,1024]{3,2,1,0:T(8,128)S(1)} %get-tuple-element.33.halo, bf16[2,416,256]{2,1,0:T(8,128)(2,1)S(1)} %get-tuple-element.34.mat1, bf16[2,320,208]{2,1,0:T(8,128)(2,1)S(1)} %get-tuple-element.35.mat2, f32[2,208,128]{2,1,0:T(8,128)S(1)} %get-tuple-element.36.diff, ...), custom_call_target="tpu_custom_call" | custom-call | tf_op jit(solution)/shard_map/cond/branch_0_fun/model/pallas_call | solution.py:390
Async XLA Ops:
  6.5 89.9 %copy-start.4 = (f32[20]{0:T(128)S(1)}, f32[20]{0:T(128)}, u32[]{:S(2)}) copy-start(f32[20]{0:T(128)} %param.12) | copy-start | bytes 244
  6.5 89.9 %copy-start = (f32[4,20,8,1024]{3,2,1,0:T(8,128)S(1)}, f32[4,20,8,1024]{3,2,1,0:T(8,128)}, u32[]{:S(2)}) copy-start(f32[4,20,8,1024]{3,2,1,0:T(8,128)} %pert.1) | copy-start | bytes 7864324
  6.5 89.9 %copy-start.1 = (s32[8,1024]{1,0:T(8,128)S(1)}, s32[8,1024]{1,0:T(8,128)}, u32[]{:S(2)}) copy-start(s32[8,1024]{1,0:T(8,128)} %mask.1) | copy-start | bytes 98308
  6.5 89.9 %copy-start.2 = (f32[20,20]{1,0:T(8,128)S(1)}, f32[20,20]{1,0:T(8,128)}, u32[]{:S(2)}) copy-start(f32[20,20]{1,0:T(8,128)} %coupling.1) | copy-start | bytes 4804
  6.5 89.9 %copy-start.3 = (s32[4]{0:T(128)S(1)}, s32[4]{0:T(128)}, u32[]{:S(2)}) copy-start(s32[4]{0:T(128)} %parents.1) | copy-start | bytes 52

commit v3 on v2

v3 whole, which is shorter than its diff:
```python
import functools
import jax
import jax.numpy as jnp
from jax import lax
from jax.experimental import pallas as pl
from jax.experimental.pallas import tpu as pltpu
from jax.sharding import PartitionSpec as P

MESH = pl.DeviceIdType.MESH
CH, LON, ROWS = 20, 1024, 8
GROUP = 5
HALF = 16
CAPS = (5, 6, 7, 8, 16)
CHUNKS = 8
WIDTH = LON // CHUNKS
EARLY = 2
AHEAD = 3
LZ, LX = 2, 1
WIN = 24


def remote(src, dst, ss, rs, dev):
    return pltpu.make_async_remote_copy(
        src_ref=src, dst_ref=dst, send_sem=ss, recv_sem=rs, device_id=dev, device_id_type=MESH
    )


def lon(k):
    return pl.ds(k * WIDTH, WIDTH)


def chan(g):
    return pl.ds(g * GROUP, GROUP)


def where_am_i():
    p, dom = lax.axis_index("particle"), lax.axis_index("domain")
    x, h = lax.div(p, 2), lax.rem(p, 2)
    peer_x = [lax.rem(x + d, 4) for d in range(4)]
    peers = [(peer_x[d] * 2 + h, dom) for d in range(4)]
    partner = (x * 2 + 1 - h, dom)
    below, above = (p, lax.rem(dom + 31, 32)), (p, lax.rem(dom + 1, 32))
    return dom, x, h, peer_x, peers, partner, below, above


def meet(devices):
    barrier = pltpu.get_barrier_semaphore()
    for dev in devices:
        pl.semaphore_signal(barrier, inc=1, device_id=dev, device_id_type=MESH)
    pl.semaphore_wait(barrier, len(devices))


def spread(states, mine, k, x, peer_x, peers, ss, rs):
    return [
        remote(
            states.at[:, chan(peer_x[d]), :, lon(k)],
            mine[k].at[pl.ds(x * 4, 4)],
            ss.at[k, d - 1],
            rs.at[k, d - 1],
            peers[d],
        )
        for d in range(1, 4)
    ]


def keep(states, mine, k, x, sem):
    return pltpu.make_async_copy(
        states.at[:, chan(x), :, lon(k)], mine[k].at[pl.ds(x * 4, 4)], sem.at[k]
    )


def wait_rows(dom, copies):
    down, up = copies
    pl.when(dom < 31)(down.wait_recv)
    pl.when(dom > 0)(up.wait_recv)


def wait_rows_sent(dom, copies):
    down, up = copies
    pl.when(dom > 0)(down.wait_send)
    pl.when(dom < 31)(up.wait_send)


def plan(states, parents, *refs):
    mine, refs = refs[:EARLY], refs[EARLY:]
    sel, listed, branch, *refs = refs
    par_send, par_x, par_z, par_xs, par_zs, bits, table, *sems = refs
    s_x1, r_x1, l_x1, s_p, r_p, s_q, r_q, l_c = sems
    _, x, h, peer_x, peers, partner, _, _ = where_am_i()
    own = [keep(states, mine, k, x, l_x1) for k in range(EARLY)]
    for c in own:
        c.start()
    lane = lax.broadcasted_iota(jnp.int32, (8, 128), 1)
    row = jnp.zeros((8, 128), jnp.int32)
    for i in range(4):
        row = jnp.where(lane == i, parents[i], row)
    par_send[...] = row
    par_x[pl.ds(x, 1)] = row[None]
    meet(peers[1:] + [partner])

    par = [remote(par_send, par_x.at[x], s_p.at[d - 1], r_p.at[d - 1], peers[d]) for d in range(1, 4)]
    first = sum((spread(states, mine, k, x, peer_x, peers, s_x1, r_x1) for k in range(EARLY)), [])
    for c in par + first:
        c.start()
    for c in par:
        c.wait_recv()
    par2 = remote(par_x, par_z, s_q.at[0], r_q.at[0], partner)
    par2.start()
    to_smem = pltpu.make_async_copy(par_x, par_xs, l_c.at[0])
    to_smem.start()

    def set_bit(i, b):
        bits[i] = b
        return b + b

    lax.fori_loop(0, 32, set_bit, jnp.int32(1))
    to_smem.wait()

    def union(ref):
        return lax.fori_loop(
            0, HALF, lambda i, m: m | bits[ref[lax.div(i, 4), 0, lax.rem(i, 4)]], jnp.int32(0), unroll=4
        )

    def member(l, half):
        return lax.div(l, 4) * 8 + half * 4 + lax.rem(l, 4)

    wanted_here = union(par_xs)

    def arrivals(l, count):
        here, there = member(l, h), member(l, 1 - h)
        table[here] = l
        table[there] = HALF + jnp.minimum(count, HALF - 1)
        return count + (lax.shift_right_logical(wanted_here, there) & 1)

    zero = jnp.int32(0)
    n_in = lax.fori_loop(0, HALF, arrivals, zero, unroll=4)

    def choose(i, carry):
        sel[i] = table[par_xs[lax.div(i, 4), 0, lax.rem(i, 4)]]
        return carry

    lax.fori_loop(0, HALF, choose, 0, unroll=4)
    par2.wait_recv()
    to_smem2 = pltpu.make_async_copy(par_z, par_zs, l_c.at[1])
    to_smem2.start()
    to_smem2.wait()
    wanted_there = union(par_zs)

    def departures(l, carry):
        count, out = carry
        bit = lax.shift_right_logical(wanted_there, member(l, h)) & 1
        out = tuple(
            jnp.where((bit == 1) & (count == c), l, old) for c, old in enumerate(out)
        )
        return count + bit, out

    n_out, out = lax.fori_loop(0, HALF, departures, (zero, (zero,) * HALF), unroll=4)
    for c in range(HALF):
        listed[c] = out[c]
    most = jnp.maximum(n_out, n_in)
    branch[0] = sum((most > cap).astype(jnp.int32) for cap in CAPS[:-1])
    for c in own:
        c.wait()
    for c in par + first:
        c.wait_send()
    for c in first:
        c.wait_recv()
    par2.wait_send()


def planned(states, parents):
    dma = pltpu.SemaphoreType.DMA
    vmem = pl.BlockSpec(memory_space=pltpu.VMEM)
    smem = pl.BlockSpec(memory_space=pltpu.SMEM)
    hbm = pl.BlockSpec(memory_space=pl.ANY)
    shape = jax.ShapeDtypeStruct
    ints = lambda *s: pltpu.SMEM(s, jnp.int32)
    return pl.pallas_call(
        plan,
        name="plan",
        out_shape=[shape((HALF, GROUP, ROWS, WIDTH), jnp.float32)] * EARLY
        + [
            shape((HALF,), jnp.int32),
            shape((HALF,), jnp.int32),
            shape((1,), jnp.int32),
        ],
        in_specs=[hbm, smem],
        out_specs=[vmem] * EARLY + [smem] * 3,
        scratch_shapes=[
            pltpu.VMEM((8, 128), jnp.int32),
            pltpu.VMEM((4, 8, 128), jnp.int32),
            pltpu.VMEM((4, 8, 128), jnp.int32),
            ints(4, 8, 128),
            ints(4, 8, 128),
            ints(32),
            ints(32),
            dma((EARLY, 3)),
            dma((EARLY, 3)),
            dma((EARLY,)),
            dma((3,)),
            dma((3,)),
            dma((1,)),
            dma((1,)),
            dma((2,)),
        ],
        compiler_params=pltpu.CompilerParams(
            collective_id=0, has_side_effects=True, vmem_limit_bytes=48 << 20
        ),
    )(states, parents)


def route(cap, states, pert, sel, listed, mask, coupling, diffusivity, *refs):
    mine, refs = refs[:EARLY], refs[EARLY:]
    res, halo, mat1, mat2, diff, land, *refs = refs
    it = iter(refs)
    take = lambda n: [next(it) for _ in range(n)]
    mine = list(mine) + take(CHUNKS - EARLY)
    crossing, crossed, back, got, edge = (take(CHUNKS) for _ in range(5))
    pert_v, strip, mask_halo = take(3)
    s_x1, r_x1, l_x1, s_z, r_z, s_x2, r_x2, s_h, r_h, s_m, r_m, l_c = it
    dom, x, h, peer_x, peers, partner, below, above = where_am_i()
    own = {k: keep(states, mine, k, x, l_x1) for k in range(EARLY, CHUNKS)}
    for c in own.values():
        c.start()
    pert_copy = pltpu.make_async_copy(pert, pert_v, l_c.at[0])
    pert_copy.start()

    @pl.when(dom == 0)
    def _():
        halo[0] = jnp.zeros(halo.shape[1:], jnp.float32)
        mask_halo[0] = jnp.zeros(mask_halo.shape[1:], jnp.int32)

    @pl.when(dom == 31)
    def _():
        halo[1] = jnp.zeros(halo.shape[1:], jnp.float32)
        mask_halo[1] = jnp.zeros(mask_halo.shape[1:], jnp.int32)

    masks = [
        remote(mask, mask_halo.at[1], s_m.at[0], r_m.at[0], below),
        remote(mask, mask_halo.at[0], s_m.at[1], r_m.at[1], above),
    ]
    sent = []

    def go(copies):
        for c in copies:
            c.start()
        sent.extend(copies)
        return copies

    def stage_z(k):
        def body(c, carry):
            crossing[k][c] = mine[k][listed[c]]
            return carry

        lax.fori_loop(0, cap, body, 0)

    stage_z(0)
    meet(peers[1:] + [partner, below, above])
    x1 = lambda k: go(spread(states, mine, k, x, peer_x, peers, s_x1, r_x1))
    first = {}
    res4 = res.reshape(4, CH, ROWS, LON)
    strip4 = strip.reshape(4, CH, ROWS, WIDTH)
    z, second, halos = {}, {}, {}
    for t in range(CHUNKS + LZ + LX):
        if t < CHUNKS:
            k = t
            if k >= EARLY:
                own[k].wait()
                for c in first[k]:
                    c.wait_recv()
            if k:
                stage_z(k)
            z[k] = go([remote(crossing[k], crossed[k], s_z.at[k], r_z.at[k], partner)])
            for j in range(EARLY, AHEAD + 1) if k == 0 else [k + AHEAD]:
                if j < CHUNKS:
                    first[j] = x1(j)
        if t == 0:
            pl.when(dom > 0)(masks[0].start)
            pl.when(dom < 31)(masks[1].start)
        if t == 1:
            for odd in range(2):
                build(coupling[...], diffusivity[...], odd, mat1, mat2, diff)
            wait_rows(dom, masks)
            sea = mask[...].astype(jnp.float32)
            for c in range(CH):
                land[pl.ds(c * ROWS, ROWS)] = sea
            low = mask_halo[0, ROWS - 1 : ROWS].astype(jnp.float32)
            high = mask_halo[1, 0:1].astype(jnp.float32)
            land[pl.ds(INNER, WIN)] = jnp.broadcast_to(low, (WIN, LON))
            land[pl.ds(INNER + WIN, WIN)] = jnp.broadcast_to(high, (WIN, LON))
        if LZ <= t < CHUNKS + LZ:
            k = t - LZ
            z[k][0].wait_recv()
            second[k] = []
            for d in (1, 2, 3, 0):

                def stage_x(j, carry, k=k, d=d):
                    s = sel[peer_x[d] * 4 + j]
                    far = s >= HALF
                    a = mine[k][jnp.where(far, 0, s)]
                    b = crossed[k][jnp.where(far, s - HALF, 0)]
                    v = jnp.where(far, b, a)
                    if d == 0:
                        got[k][x, j] = v
                    else:
                        back[k][d - 1, j] = v
                    return carry

                lax.fori_loop(0, 4, stage_x, 0)
                if d:
                    second[k] += go(
                        [
                            remote(
                                back[k].at[d - 1],
                                got[k].at[x],
                                s_x2.at[k, d - 1],
                                r_x2.at[k, d - 1],
                                peers[d],
                            )
                        ]
                    )
        if t >= LZ + LX:
            k = t - LZ - LX
            if k == 0:
                pert_copy.wait()
            for c in second[k]:
                c.wait_recv()
            for g in range(4):
                new = got[k][g] + pert_v[:, chan(g), :, lon(k)]
                res4[:, chan(g), :, lon(k)] = new
                strip4[:, chan(g)] = new
            for i, r in enumerate((0, 1, 6, 7)):
                edge[k][i // 2, i % 2] = strip[pl.ds(r, 4 * CH, stride=ROWS)]
            halos[k] = [
                remote(edge[k].at[0], halo.at[1, :, :, lon(k)], s_h.at[k, 0], r_h.at[k, 0], below),
                remote(edge[k].at[1], halo.at[0, :, :, lon(k)], s_h.at[k, 1], r_h.at[k, 1], above),
            ]
            pl.when(dom > 0)(halos[k][0].start)
            pl.when(dom < 31)(halos[k][1].start)
    for k in range(CHUNKS):
        wait_rows(dom, halos[k])
    for c in sent:
        c.wait_send()
    for copies in [masks] + [halos[k] for k in range(CHUNKS)]:
        wait_rows_sent(dom, copies)


def routed(cap, states, pert, sel, listed, mask, coupling, diffusivity, *mine):
    dma = pltpu.SemaphoreType.DMA
    vm = lambda *s: pltpu.VMEM(s, jnp.float32)
    vmem = pl.BlockSpec(memory_space=pltpu.VMEM)
    smem = pl.BlockSpec(memory_space=pltpu.SMEM)
    hbm = pl.BlockSpec(memory_space=pl.ANY)
    scratch = [vm(HALF, GROUP, ROWS, WIDTH)] * (CHUNKS - EARLY)
    for lead in ((cap,), (cap,), (3, 4), (4, 4)):
        scratch += [vm(*lead, GROUP, ROWS, WIDTH)] * CHUNKS
    scratch += [vm(2, 2, 4 * CH, WIDTH)] * CHUNKS
    scratch += [vm(4, CH, ROWS, LON), vm(4 * CH * ROWS, WIDTH)]
    scratch += [pltpu.VMEM((2, ROWS, LON), jnp.int32)]
    three, two, one = dma((CHUNKS, 3)), dma((CHUNKS, 2)), dma((CHUNKS,))
    scratch += [three, three, one, one, one, three, three, two, two, dma((2,)), dma((2,)), dma((1,))]
    return pl.pallas_call(
        functools.partial(route, cap),
        name=f"route{cap}",
        out_shape=(
            jax.ShapeDtypeStruct((4 * CH * ROWS, LON), jnp.float32),
            jax.ShapeDtypeStruct((2, 2, 4 * CH, LON), jnp.float32),
            jax.ShapeDtypeStruct((2, 2 * MIDDLE, OUTER), jnp.bfloat16),
            jax.ShapeDtypeStruct((2, 2 * INNER, MIDDLE), jnp.bfloat16),
            jax.ShapeDtypeStruct((2, MIDDLE, 128), jnp.float32),
            jax.ShapeDtypeStruct((MIDDLE, LON), jnp.float32),
        ),
        in_specs=[hbm, hbm, smem, smem] + [vmem] * (3 + EARLY),
        out_specs=(vmem,) * 6,
        scratch_shapes=scratch,
        compiler_params=pltpu.CompilerParams(
            collective_id=1 + CAPS.index(cap), has_side_effects=True, vmem_limit_bytes=48 << 20
        ),
    )(states, pert, sel, listed, mask, coupling, diffusivity, *mine)


INNER = CH * ROWS
MIDDLE = INNER + 2 * WIN
OUTER = INNER + 4 * WIN


def place(i, off):
    q = i - INNER
    window = (q >= WIN).astype(jnp.int32) + (q >= 2 * WIN) + (q >= 3 * WIN)
    inside = i < INNER
    ch = jnp.where(inside, i >> 3, q - window * WIN - off)
    outer_row = jnp.where(window == 0, -1, jnp.where(window == 1, 8, jnp.where(window == 2, -2, 9)))
    return ch, jnp.where(inside, i & 7, outer_row)


def stencil(coupling, diffusivity, rows, cols, off):
    high = functools.partial(jnp.dot, preferred_element_type=jnp.float32, precision=lax.Precision.HIGHEST)
    ch_a, _ = place(lax.broadcasted_iota(jnp.int32, (rows, CH), 0), off)
    pick_a = (ch_a == lax.broadcasted_iota(jnp.int32, (rows, CH), 1)).astype(jnp.float32)
    ch_b, _ = place(lax.broadcasted_iota(jnp.int32, (CH, cols), 1), off)
    pick_b = (ch_b == lax.broadcasted_iota(jnp.int32, (CH, cols), 0)).astype(jnp.float32)
    full = high(high(pick_a, coupling), pick_b)
    d = jnp.sum(pick_a * diffusivity, axis=1, keepdims=True)
    shape = (rows, cols)
    ci, ri = place(lax.broadcasted_iota(jnp.int32, shape, 0), off)
    cj, rj = place(lax.broadcasted_iota(jnp.int32, shape, 1), off)
    real = (ci >= 0) & (ci < CH) & (cj >= 0) & (cj < CH)
    gap = ri - rj
    vertical = jnp.where(gap == 0, -4.0, jnp.where((gap == 1) | (gap == -1), 1.0, 0.0))
    m = jnp.where(gap == 0, full, 0.0) + jnp.where(ci == cj, vertical * d, 0.0)
    return jnp.where(real, m, 0.0), d


def halves(v):
    top = v.astype(jnp.bfloat16)
    return top, (v - top.astype(jnp.float32)).astype(jnp.bfloat16)


def apply(mat, v):
    dot = functools.partial(jnp.dot, preferred_element_type=jnp.float32)
    top, low = halves(v)
    n = mat.shape[0] // 2
    both = dot(mat[...], top)
    return both[:n] + both[n:] + dot(mat[:n], low)


def build(coupling, diffusivity, odd, mat1, mat2, diff):
    m, d = stencil(coupling, diffusivity, MIDDLE, OUTER, 4 * odd)
    top, low = halves(m)
    mat1[odd, :MIDDLE] = top
    mat1[odd, MIDDLE:] = low
    diff[odd] = jnp.broadcast_to(d, (MIDDLE, 128))
    m, _ = stencil(coupling, diffusivity, INNER, MIDDLE, 4 * odd)
    top, low = halves(m)
    mat2[odd, :INNER] = top
    mat2[odd, INNER:] = low


def sides(v):
    return pltpu.roll(v, 1, 1) + pltpu.roll(v, LON - 1, 1)


def model(res, halo, mat1, mat2, diff, land, out):
    j = pl.program_id(0)

    odd = lax.rem(j, 2)
    start = pl.multiple_of(lax.div(j, 2) * 40 + odd * 16, 8)
    rows = pl.ds(start, WIN)
    v = jnp.concatenate(
        [
            res[0],
            halo[0, 1, rows],
            halo[1, 0, rows],
            halo[0, 0, rows],
            halo[1, 1, rows],
        ],
        axis=0,
    )
    d = diff[odd][:, :1]
    u = v[:MIDDLE]
    first = u + land[...] * (apply(mat1.at[odd], v) + d * sides(u))
    inner = first[:INNER]
    out[0] = inner + land[:INNER] * (apply(mat2.at[odd], first) + d[:INNER] * sides(inner))


def modelled(res, halo, mat1, mat2, diff, land):
    whole = pl.BlockSpec(memory_space=pltpu.VMEM)
    block = pl.BlockSpec((1, INNER, LON), lambda j: (j, 0, 0))
    return pl.pallas_call(
        model,
        name="model",
        grid=(4,),
        out_shape=pltpu.HBM((4, INNER, LON), jnp.float32),
        in_specs=[block, whole, whole, whole, whole, whole],
        out_specs=block,
        compiler_params=pltpu.CompilerParams(vmem_limit_bytes=48 << 20),
    )(res, halo, mat1, mat2, diff, land)


def on_device(states, parents, perturbation, sea_mask, diffusivity, coupling):
    *mine, sel, listed, branch = planned(states, parents)
    res, *others = lax.switch(
        branch[0],
        [functools.partial(routed, cap) for cap in CAPS],
        states,
        perturbation,
        sel,
        listed,
        sea_mask,
        coupling,
        diffusivity[None],
        *mine,
    )
    return modelled(res.reshape(4, INNER, LON), *others).reshape(4, CH, ROWS, LON)


def solution(mesh):
    in_specs = (
        P("particle", None, "domain", None),
        P("particle"),
        P("particle", None, "domain", None),
        P("domain", None),
        P(),
        P(),
    )
    out_specs = P("particle", None, "domain", None)
    return jax.shard_map(
        on_device, mesh=mesh, in_specs=in_specs, out_specs=out_specs, check_vma=False
    )
```

time: 110 us -> 88.9 us (0.81)
  between operations: 14.1 us -> 0.67 us
  Pallas kernels: 94.8 us -> 86.8 us
    pallas_call x1 -> x2, Pallas kernels: 89.1 us -> 81.1 us  [the longest x1 62.8 us: routed(): pl.pallas_call(functools.partial(route, cap), name=f'route{cap}', out_sha...]
where the time goes in v3:
time: 88.9 us; the launch traced here: 88.4 us
  Pallas kernels  86.8 us (98%)
    pallas_call x1, Pallas kernels, routed(): pl.pallas_call(functools.partial(route, cap), name=f'route{cap}', out_sha...  62.8 us
    pallas_call x1, Pallas kernels, planned(): pl.pallas_call(plan, name='plan', out_shape=[shape((HALF, GROUP, ROWS, WI...  18.3 us
    pallas_call x1, Pallas kernels, modelled(): pl.pallas_call(model, name='model', grid=(4,), out_shape=pltpu.HBM((4, IN...  5.71 us

profile of v3, /device:TPU:25, one launch (start us, length us, event | category | flops | bytes accessed | tf_op | source)
XLA Modules:
  0.0 88.4 jit_solution(2272637344165922761)
XLA Ops:
  0.0 0.0 copy-start.3
  0.0 0.0 copy-start
  0.0 0.7 copy-done
  0.7 0.0 copy-start.1
  0.7 0.0 copy-start.2
  0.7 18.3 %plan.1 = (f32[16,5,8,128]{3,2,1,0:T(8,128)S(1)}, f32[16,5,8,128]{3,2,1,0:T(8,128)S(1)}, s32[16]{0:T(128)S(1)}, s32[16]{0:T(128)S(1)}, s32[1]{0:T(128)}) custom-call(f32[4,20,8,1024]{3,2,1,0:T(8,128)} %states.1, s32[4]{0:T(128)S(1)} %copy-done), custom_call_target="tpu_custom_call" | custom-call | tf_op jit(solution)/shard_map/plan/pallas_call | solution.py:178
  19.6 0.0 copy-done.3
  19.6 0.0 copy-done.1
  19.6 0.0 copy-done.2
  19.6 63.0 %conditional.1 = ((f32[640,1024]{1,0:T(8,128)S(1)}, f32[2,2,80,1024]{3,2,1,0:T(8,128)S(1)}, bf16[2,416,256]{2,1,0:T(8,128)(2,1)S(1)}, bf16[2,320,208]{2,1,0:T(8,...) conditional(s32[]{:T(128)} %bitcast, ...), branch_computations={%region_0.0_spmd, %region_1.0_spmd, %region_2.0_spmd, %region_3.0_... | conditional | bytes 8 | solution.py:482
  19.6 62.8 %route5.1 = (f32[640,1024]{1,0:T(8,128)S(1)}, f32[2,2,80,1024]{3,2,1,0:T(8,128)S(1)}, bf16[2,416,256]{2,1,0:T(8,128)(2,1)S(1)}, bf16[2,320,208]{2,1,0:T(8,128)(2...) custom-call(f32[4,20,8,1024]{3,2,1,0:T(8,128)S(1)} %get-tuple-element.133.states, ...), custom_call_target="tpu_custom_call" | custom-call | tf_op jit(solution)/shard_map/cond/branch_0_fun/route5/pallas_call | solution.py:362
  82.7 5.7 %model.1 = f32[4,160,1024]{2,1,0:T(8,128)} custom-call(f32[4,160,1024]{2,1,0:T(8,128)S(1)} %bitcast.4, f32[2,2,80,1024]{3,2,1,0:T(8,128)S(1)} %get-tuple-element.237.halo, bf16[2,416,256]{2,1,0:T(8,128)(2,1)S(1)} %get-tuple-element.236.mat1, bf16[2,320,208]{2,1,0:T(8,128)(2,1)S(1)} %get-tuple-element.235.mat2, f32[2,208,128]{2,1,0:T(8,128)S(1)} %get-tuple-element.234.diff, ...), custom_call_target="tpu_custom_call" | custom-call | tf_op jit(solution)/shard_map/model/pallas_call | solution.py:469
Async XLA Ops:
  0.0 19.6 %copy-start.3 = (f32[20]{0:T(128)S(1)}, f32[20]{0:T(128)}, u32[]{:S(2)}) copy-start(f32[20]{0:T(128)} %param.15) | copy-start | bytes 244
  0.0 0.7 copy-start
  0.7 18.9 %copy-start.1 = (f32[4,20,8,1024]{3,2,1,0:T(8,128)S(1)}, f32[4,20,8,1024]{3,2,1,0:T(8,128)}, u32[]{:S(2)}) copy-start(f32[4,20,8,1024]{3,2,1,0:T(8,128)} %states.1) | copy-start | bytes 7864324
  0.7 18.9 %copy-start.2 = (f32[20,20]{1,0:T(8,128)S(1)}, f32[20,20]{1,0:T(8,128)}, u32[]{:S(2)}) copy-start(f32[20,20]{1,0:T(8,128)} %param.16) | copy-start | bytes 4804

commit v4 on v3

--- a/solution.py
+++ b/solution.py
@@ -14,8 +14,8 @@
 CHUNKS = 8
 WIDTH = LON // CHUNKS
 EARLY = 2
-AHEAD = 3
-LZ, LX = 2, 1
+AHEAD = 2
+LZ, LX = 2, 2
 WIN = 24
 
 

time: 88.9 us -> 89.2 us (level)
  the two profiles are of different devices: /device:TPU:25 before, /device:TPU:64 now
where the time goes in v4:
time: 89.2 us; the launch traced here: 89 us
  Pallas kernels  87.4 us (98%)
    pallas_call x1, Pallas kernels, routed(): pl.pallas_call(functools.partial(route, cap), name=f'route{cap}', out_sha...  64.2 us
    pallas_call x1, Pallas kernels, planned(): pl.pallas_call(plan, name='plan', out_shape=[shape((HALF, GROUP, ROWS, WI...  17.6 us
    pallas_call x1, Pallas kernels, modelled(): pl.pallas_call(model, name='model', grid=(4,), out_shape=pltpu.HBM((4, IN...  5.7 us

profile of v4, /device:TPU:64, one launch (start us, length us, event | category | flops | bytes accessed | tf_op | source)
XLA Modules:
  0.0 89.0 jit_solution(5516618964510999900)
XLA Ops:
  0.0 0.0 copy-start.3
  0.0 0.0 copy-start
  0.0 0.7 copy-done
  0.7 0.0 copy-start.1
  0.7 0.0 copy-start.2
  0.7 17.6 %plan.1 = (f32[16,5,8,128]{3,2,1,0:T(8,128)S(1)}, f32[16,5,8,128]{3,2,1,0:T(8,128)S(1)}, s32[16]{0:T(128)S(1)}, s32[16]{0:T(128)S(1)}, s32[1]{0:T(128)}) custom-call(f32[4,20,8,1024]{3,2,1,0:T(8,128)} %states.1, s32[4]{0:T(128)S(1)} %copy-done), custom_call_target="tpu_custom_call" | custom-call | tf_op jit(solution)/shard_map/plan/pallas_call | solution.py:178
  18.9 0.0 copy-done.3
  18.9 0.0 copy-done.1
  18.9 0.0 copy-done.2
  18.9 64.4 %conditional.1 = ((f32[640,1024]{1,0:T(8,128)S(1)}, f32[2,2,80,1024]{3,2,1,0:T(8,128)S(1)}, bf16[2,416,256]{2,1,0:T(8,128)(2,1)S(1)}, bf16[2,320,208]{2,1,0:T(8,...) conditional(s32[]{:T(128)} %bitcast, ...), branch_computations={%region_0.0_spmd, %region_1.0_spmd, %region_2.0_spmd, %region_3.0_... | conditional | bytes 8 | solution.py:482
  18.9 64.2 %route5.1 = (f32[640,1024]{1,0:T(8,128)S(1)}, f32[2,2,80,1024]{3,2,1,0:T(8,128)S(1)}, bf16[2,416,256]{2,1,0:T(8,128)(2,1)S(1)}, bf16[2,320,208]{2,1,0:T(8,128)(2...) custom-call(f32[4,20,8,1024]{3,2,1,0:T(8,128)S(1)} %get-tuple-element.133.states, ...), custom_call_target="tpu_custom_call" | custom-call | tf_op jit(solution)/shard_map/cond/branch_0_fun/route5/pallas_call | solution.py:362
  83.3 5.7 %model.1 = f32[4,160,1024]{2,1,0:T(8,128)} custom-call(f32[4,160,1024]{2,1,0:T(8,128)S(1)} %bitcast.4, f32[2,2,80,1024]{3,2,1,0:T(8,128)S(1)} %get-tuple-element.237.halo, bf16[2,416,256]{2,1,0:T(8,128)(2,1)S(1)} %get-tuple-element.236.mat1, bf16[2,320,208]{2,1,0:T(8,128)(2,1)S(1)} %get-tuple-element.235.mat2, f32[2,208,128]{2,1,0:T(8,128)S(1)} %get-tuple-element.234.diff, ...), custom_call_target="tpu_custom_call" | custom-call | tf_op jit(solution)/shard_map/model/pallas_call | solution.py:469
Async XLA Ops:
  0.0 18.9 %copy-start.3 = (f32[20]{0:T(128)S(1)}, f32[20]{0:T(128)}, u32[]{:S(2)}) copy-start(f32[20]{0:T(128)} %param.15) | copy-start | bytes 244
  0.0 0.7 copy-start
  0.7 18.2 %copy-start.1 = (f32[4,20,8,1024]{3,2,1,0:T(8,128)S(1)}, f32[4,20,8,1024]{3,2,1,0:T(8,128)}, u32[]{:S(2)}) copy-start(f32[4,20,8,1024]{3,2,1,0:T(8,128)} %states.1) | copy-start | bytes 7864324
  0.7 18.2 %copy-start.2 = (f32[20,20]{1,0:T(8,128)S(1)}, f32[20,20]{1,0:T(8,128)}, u32[]{:S(2)}) copy-start(f32[20,20]{1,0:T(8,128)} %param.16) | copy-start | bytes 4804
